TPU v7x, 32 devices: a whole 2x2x4 slice. The times are simulated.
32 devices in a mesh: section: 2 (over x), dp: 16 (over z, y, core).
Axes of the slice: x: 2, y: 2, z: 4, core: 2. Of those that a mesh axis runs over, the one named last changes fastest.
Arguments:
- boundary: bfloat16 [2, 16384, 768], P('section', 'dp'), may hold values from -6 to 6
- inward: bfloat16 [2, 768, 2304], P('section'), may hold values from -0.21875 to 0.21875
- inbias: float32 [2, 2304], P('section'), may hold values from -1.5 to 1.5
- outward: bfloat16 [2, 768, 768], P('section'), may hold values from -3 to 3
- outbias: float32 [2, 768], P('section'), may hold values from -1.5 to 1.5
- normgain: float32 [2, 768], P('section'), may hold values from 0.25 to 1.75
- normshift: float32 [2, 768], P('section'), may hold values from -1.5 to 1.5
- expand: bfloat16 [2, 768, 3072], P('section'), may hold values from -0.21875 to 0.21875
- expbias: float32 [2, 3072], P('section'), may hold values from -1.5 to 1.5
- shrink: bfloat16 [2, 3072, 768], P('section'), may hold values from -0.109375 to 0.109375
- shrbias: float32 [2, 768], P('section'), may hold values from -1.5 to 1.5
- lastgain: float32 [2, 768], P('section'), may hold values from 0.25 to 1.75
- lastshift: float32 [2, 768], P('section'), may hold values from -1.5 to 1.5
Outputs:
- results: bfloat16 [2, 16384, 768], P('section', 'dp')
- inward_grads: float32 [2, 768, 2304], P('section')
- inbias_grads: float32 [2, 2304], P('section')
- outward_grads: float32 [2, 768, 768], P('section')
- outbias_grads: float32 [2, 768], P('section')
- normgain_grads: float32 [2, 768], P('section')
- normshift_grads: float32 [2, 768], P('section')
- expand_grads: float32 [2, 768, 3072], P('section')
- expbias_grads: float32 [2, 3072], P('section')
- shrink_grads: float32 [2, 3072, 768], P('section')
- shrbias_grads: float32 [2, 768], P('section')
- lastgain_grads: float32 [2, 768], P('section')
- lastshift_grads: float32 [2, 768], P('section')
All inputs are finite; a program needn't handle non-finite values.
Results may differ from a plain program's by a relative error of at most 0.014.
Values may be sent and summed in bfloat16 or wider, within the bound.
A program may use at most 384 MiB of HBM per device.

v0:
```python
from functools import partial
import math

import jax
import jax.numpy as jnp
import numpy as np
from jax import lax
from jax.experimental import pallas as pl
from jax.experimental.pallas import tpu as pltpu
from jax.sharding import PartitionSpec as P

HEAD = 64
SEQ = 512
CHUNK = 256
PAIR = 2 * HEAD
EPSILON = 1e-05
MESH = pl.DeviceIdType.MESH
F32 = jnp.float32
BF16 = jnp.bfloat16
VMEM_BYTES = 63 * 2**20


def dot(a, b):
    return jnp.dot(a, b, preferred_element_type=F32)


def dot_nt(a, b):
    return lax.dot_general(a, b, (((1,), (1,)), ((), ())), preferred_element_type=F32)


def dot_tn(a, b):
    return lax.dot_general(a, b, (((0,), (0,)), ((), ())), preferred_element_type=F32)


def softplus(p):
    return jnp.maximum(p, 0.0) + jnp.log1p(jnp.exp(-jnp.abs(p)))


def sigmoid_of_softplus(q):
    series = q * (1.0 - q * (0.5 - q * (1.0 / 6.0 - q * (1.0 / 24.0))))
    return jnp.where(q < 0.03, series, 1.0 - jnp.exp(-q))


def cosine_tables():
    step = math.pi / (2.0 * SEQ)
    i = np.arange(CHUNK)[:, None]
    j = np.arange(CHUNK)[None, :]
    near = np.where(i >= j, np.cos((i - j) * step), 0.0).astype(np.float32)
    far = np.cos((i - j + CHUNK) * step).astype(np.float32)
    return near, far


def lane_masks():
    lanes = np.arange(PAIR)
    return np.stack([lanes < HEAD, lanes >= HEAD])[:, None, :].astype(np.float32)


def layer_kernel(
    boundary, inward, outward, expand, shrink,
    inbias, outbias, normgain, normshift, expbias, shrbias, lastgain, lastshift,
    near, far, masks,
    results, f_x, f_a, f_h, f_g, f_p, f_o, f_u, f_f, vector_rows,
    win, wout, wexp, wshr,
    xs, qkv, att, low, zin, hbs, gs, gps, n1s, n2s, s1s, s2s, dys, ybuf, xbuf,
    acc, keep, das, carry, vectors,
    load_sems, out_sems, res_sems, fwd_send, fwd_recv, bwd_send, bwd_recv,
):
    rows_all, width = xs.shape
    hidden = wexp.shape[1]
    chunks = rows_all // CHUNK
    pairs = width // PAIR
    slabs = hidden // width
    section = lax.axis_index("section")
    first = section == 0
    peer = {"section": 1 - section}

    loads = [
        pltpu.make_async_copy(src, dst, load_sems.at[i])
        for i, (src, dst) in enumerate(
            [(inward, win), (outward, wout), (expand, wexp), (shrink, wshr)]
        )
    ]
    load_x = pltpu.make_async_copy(boundary, xs, load_sems.at[4])
    load_y = pltpu.make_async_copy(boundary, dys, load_sems.at[4])

    loads[0].start()

    @pl.when(first)
    def _():
        load_x.start()

    @pl.when(jnp.logical_not(first))
    def _():
        load_y.start()

    barrier = pltpu.get_barrier_semaphore()
    pl.semaphore_signal(barrier, inc=1, device_id=peer, device_id_type=MESH)
    vectors[...] = jnp.zeros_like(vectors)
    pl.semaphore_wait(barrier, 1)

    def rows_of(c):
        return pl.ds(pl.multiple_of(c * CHUNK, CHUNK), CHUNK)

    def send_forward(c):
        return pltpu.make_async_remote_copy(
            src_ref=ybuf.at[rows_of(c)], dst_ref=xs.at[rows_of(c)],
            send_sem=fwd_send.at[c], recv_sem=fwd_recv.at[c],
            device_id=peer, device_id_type=MESH,
        )

    def send_backward(c):
        return pltpu.make_async_remote_copy(
            src_ref=xbuf.at[rows_of(c)], dst_ref=dys.at[rows_of(c)],
            send_sem=bwd_send.at[c], recv_sem=bwd_recv.at[c],
            device_id=peer, device_id_type=MESH,
        )

    def result_copy(buf, c):
        return pltpu.make_async_copy(buf.at[rows_of(c)], results.at[rows_of(c)], res_sems.at[c])

    early = [(xs, f_x), (att, f_a), (hbs, f_h), (gs, f_g)]
    late = [(qkv, f_p), (n1s, f_o), (gps, f_u), (n2s, f_f)]

    def factor_copies(c, which, base):
        return [
            pltpu.make_async_copy(src.at[rows_of(c)], dst.at[rows_of(c)], out_sems.at[c, base + i])
            for i, (src, dst) in enumerate(which)
        ]

    def column_sum(at, value):
        vectors[at] += jnp.sum(value, axis=0, keepdims=True)

    def norm_forward(e):
        mean = jnp.mean(e, axis=-1, keepdims=True)
        center = e - mean
        s = lax.rsqrt(jnp.mean(center * center, axis=-1, keepdims=True) + EPSILON)
        return center * s, s

    def norm_backward(dn, n, s):
        m1 = jnp.mean(dn, axis=-1, keepdims=True)
        m2 = jnp.mean(dn * n, axis=-1, keepdims=True)
        return s * (dn - m1 - n * m2)

    def pair_columns(hp):
        return [pl.ds(pl.multiple_of(i * width + hp * PAIR, PAIR), PAIR) for i in range(3)]

    def attend(c, wide):
        rows = rows_of(c)
        tiles = [(rows, near)] + ([(rows_of(c - 1), far)] if wide else [])
        m = [masks[a].astype(BF16) for a in range(2)]

        def one_pair(hp, _):
            cq, ck, cv = pair_columns(hp)
            q = qkv[rows, cq]
            nz = None
            for key_rows, weights in tiles:
                k, v = qkv[key_rows, ck], qkv[key_rows, cv]
                for a in range(2):
                    s = (dot_nt(q * m[a], k) * weights[...]).astype(BF16)
                    right = jnp.concatenate(
                        [v * m[a], jnp.broadcast_to(m[a], v.shape)], axis=1
                    )
                    part = dot(s, right)
                    nz = part if nz is None else nz + part
            inverse = 1.0 / nz[:, PAIR:]
            a_full = nz[:, :PAIR] * inverse
            a_high = a_full.astype(BF16)
            att[rows, cq] = a_high
            low[rows, cq] = (a_full - a_high.astype(F32)).astype(BF16)
            zin[rows, cq] = inverse.astype(BF16)
            return 0

        lax.fori_loop(0, pairs, one_pair, 0, unroll=True)

    def attend_backward(c, wide):
        rows = rows_of(c)
        m = [masks[a].astype(BF16) for a in range(2)]
        left = lax.broadcasted_iota(jnp.int32, (CHUNK, PAIR), 1) < HEAD

        def one_pair(hp, _):
            cq, ck, cv = pair_columns(hp)
            q, k, v = qkv[rows, cq], qkv[rows, ck], qkv[rows, cv]
            dn = (das[:, cq].astype(F32) * zin[rows, cq].astype(F32)).astype(BF16)
            prod = dn.astype(F32) * (att[rows, cq].astype(F32) + low[rows, cq].astype(F32))
            dz = jnp.concatenate(
                [-jnp.sum(prod * masks[a], axis=-1, keepdims=True) for a in range(2)], axis=0
            )
            both_q = jnp.concatenate([q * m[a] for a in range(2)], axis=0)
            both_dn = jnp.concatenate([dn * m[a] for a in range(2)], axis=0)

            def tile(kt, vt, weights):
                w = jnp.concatenate([weights[...]] * 2, axis=0)
                s = (dot_nt(both_q, kt) * w).astype(BF16)
                ds = ((dot_nt(both_dn, vt) + dz) * w).astype(BF16)
                dq2 = dot(ds, kt)
                dq = jnp.where(left, dq2[:CHUNK], dq2[CHUNK:])
                return dq, dot_tn(ds, both_q), dot_tn(s, both_dn)

            dq, dk, dv = tile(k, v, near)
            wide_cols = [pl.ds(pl.multiple_of(i * width + hp * PAIR, PAIR), PAIR) for i in range(2)]
            if wide:
                kp, vp = qkv[rows_of(c - 1), ck], qkv[rows_of(c - 1), cv]
                dqp, dkp, dvp = tile(kp, vp, far)
                dq = dq + dqp
                carry[:, wide_cols[0]] = dkp
                carry[:, wide_cols[1]] = dvp
            else:
                dk = dk + carry[:, wide_cols[0]]
                dv = dv + carry[:, wide_cols[1]]
            qkv[rows, cq] = (dq * sigmoid_of_softplus(q.astype(F32))).astype(BF16)
            qkv[rows, ck] = (dk * sigmoid_of_softplus(k.astype(F32))).astype(BF16)
            qkv[rows, cv] = dv.astype(BF16)
            return 0

        lax.fori_loop(0, pairs, one_pair, 0, unroll=True)

    def forward(c, begins):
        rows = rows_of(c)

        @pl.when(begins)
        def _():
            loads[0].wait()

            @pl.when(first)
            def _():
                load_x.wait()

            for load in loads[1:]:
                load.start()

        @pl.when(jnp.logical_not(first))
        def _():
            send_forward(c).wait_recv()

        for i in range(3):
            cols = slice(i * width, (i + 1) * width)
            p = dot(xs[rows, :], win[:, cols]) + inbias[:, cols]
            qkv[rows, cols] = (softplus(p) if i < 2 else p).astype(BF16)

        @pl.when(c % 2 == 0)
        def _():
            attend(c, False)

        @pl.when(c % 2 == 1)
        def _():
            attend(c, True)

        @pl.when(begins)
        def _():
            for load in loads[1:]:
                load.wait()

        e = xs[rows, :].astype(F32) + (dot(att[rows, :], wout[...]) + outbias[...])
        n1, s1 = norm_forward(e)
        n1s[rows, :] = n1.astype(BF16)
        s1s[rows, :] = s1
        h = n1 * normgain[...] + normshift[...]
        hbs[rows, :] = h.astype(BF16)
        acc[...] = h + shrbias[...]
        for i in range(slabs):
            cols = slice(i * width, (i + 1) * width)
            u = dot(hbs[rows, :], wexp[:, cols]) + expbias[:, cols]
            phi = 0.5 * (1.0 + lax.erf(u * math.sqrt(0.5)))
            g = (u * phi).astype(BF16)
            gs[rows, cols] = g
            gps[rows, cols] = (
                phi + u * (jnp.exp(u * u * -0.5) * (1.0 / math.sqrt(2.0 * math.pi)))
            ).astype(BF16)
            acc[...] += dot(g, wshr[cols, :])
        n2, s2 = norm_forward(acc[...])
        n2s[rows, :] = n2.astype(BF16)
        s2s[rows, :] = s2
        ybuf[rows, :] = (n2 * lastgain[...] + lastshift[...]).astype(BF16)

        @pl.when(first)
        def _():
            send_forward(c).start()

        @pl.when(jnp.logical_not(first))
        def _():
            result_copy(ybuf, c).start()

        for copy in factor_copies(c, early, 0):
            copy.start()

    def backward(c):
        rows = rows_of(c)

        @pl.when(first)
        def _():
            send_backward(c).wait_recv()

        @pl.when(jnp.logical_and(jnp.logical_not(first), c == 1))
        def _():
            load_y.wait()

        dy = dys[rows, :].astype(F32)
        n2 = n2s[rows, :].astype(F32)
        column_sum(7 + slabs, dy * n2)
        column_sum(8 + slabs, dy)
        dr = norm_backward(dy * lastgain[...], n2, s2s[rows, :])
        df = dr.astype(BF16)
        n2s[rows, :] = df
        column_sum(6 + slabs, df.astype(F32))
        acc[...] = dr
        for i in range(slabs):
            cols = slice(i * width, (i + 1) * width)
            dg = dot_nt(n2s[rows, :], wshr[cols, :])
            du = (dg * gps[rows, cols].astype(F32)).astype(BF16)
            gps[rows, cols] = du
            column_sum(6 + i, du.astype(F32))
            acc[...] += dot_nt(du, wexp[:, cols])
        dh = acc[...]
        n1 = n1s[rows, :].astype(F32)
        column_sum(4, dh * n1)
        column_sum(5, dh)
        de = norm_backward(dh * normgain[...], n1, s1s[rows, :])
        keep[...] = de
        do = de.astype(BF16)
        n1s[rows, :] = do
        column_sum(3, do.astype(F32))
        das[...] = dot_nt(do, wout[...]).astype(BF16)

        @pl.when(c % 2 == 0)
        def _():
            attend_backward(c, False)

        @pl.when(c % 2 == 1)
        def _():
            attend_backward(c, True)

        for i in range(3):
            column_sum(i, qkv[rows, i * width : (i + 1) * width].astype(F32))
        dx = keep[...] + dot_nt(qkv[rows, :], win[...])
        xbuf[rows, :] = dx.astype(BF16)

        @pl.when(first)
        def _():
            result_copy(xbuf, c).start()

        @pl.when(jnp.logical_not(first))
        def _():
            send_backward(c).start()

        for copy in factor_copies(c, late, 4):
            copy.start()

    def step(t, _):
        group, place = t // 4, t % 4
        ahead = jnp.where(first, t < chunks, place < 2)
        c_forward = jnp.where(first, t, 2 * group + place)
        back = t - chunks
        c_backward = jnp.where(first, 2 * (back // 2) + 1 - back % 2, 2 * group + 3 - place)

        @pl.when(ahead)
        def _():
            forward(c_forward, t == 0)

        @pl.when(jnp.logical_not(ahead))
        def _():
            backward(c_backward)

        return 0

    lax.fori_loop(0, 2 * chunks, step, 0)
    for i in range(vectors.shape[0]):
        vector_rows[i : i + 1, :] = vectors[i]

    def finish(c, _):
        @pl.when(first)
        def _():
            send_forward(c).wait_send()
            result_copy(xbuf, c).wait()

        @pl.when(jnp.logical_not(first))
        def _():
            send_backward(c).wait_send()
            result_copy(ybuf, c).wait()

        for copy in factor_copies(c, early, 0) + factor_copies(c, late, 4):
            copy.wait()
        return 0

    lax.fori_loop(0, chunks, finish, 0)


def run_layer(boundary, weights, biases):
    rows, width = boundary.shape
    hidden = weights[2].shape[1]
    chunks = rows // CHUNK
    near, far = cosine_tables()
    masks = lane_masks()
    slabs = hidden // width
    any_space = pl.BlockSpec(memory_space=pl.ANY)
    vmem = pl.BlockSpec(memory_space=pltpu.VMEM)
    out_widths = [width] * 4 + [hidden, 3 * width, width, hidden, width]
    out_shape = [jax.ShapeDtypeStruct((rows, w), BF16) for w in out_widths]
    vector_count = -(-(9 + slabs) // 8) * 8
    out_shape.append(jax.ShapeDtypeStruct((vector_count, width), F32))
    low = lambda *shape: pltpu.VMEM(shape, BF16)
    wide = lambda *shape: pltpu.VMEM(shape, F32)
    dma = pltpu.SemaphoreType.DMA
    return pl.pallas_call(
        layer_kernel,
        out_shape=out_shape,
        in_specs=[any_space] * 5 + [vmem] * 11,
        out_specs=[any_space] * 9 + [vmem],
        scratch_shapes=[
            low(width, 3 * width), low(width, width), low(width, hidden), low(hidden, width),
            low(rows, width), low(rows, 3 * width), low(rows, width), low(rows, width),
            low(rows, width), low(rows, width), low(rows, hidden), low(rows, hidden),
            low(rows, width), low(rows, width), wide(rows, 1), wide(rows, 1),
            low(rows, width), low(rows, width), low(rows, width),
            wide(CHUNK, width), wide(CHUNK, width), low(CHUNK, width), wide(CHUNK, 2 * width),
            wide(vector_count, 1, width),
            dma((5,)), dma((chunks, 8)), dma((chunks,)), dma((chunks,)), dma((chunks,)),
            dma((chunks,)), dma((chunks,)),
        ],
        compiler_params=pltpu.CompilerParams(
            collective_id=0, has_side_effects=True, vmem_limit_bytes=VMEM_BYTES
        ),
        name="layer",
    )(boundary, *weights, *biases, jnp.asarray(near), jnp.asarray(far), jnp.asarray(masks))


SETS = 2
LANES_Z = 4

ARRIVE_Y = 2
PAIR_AT = (0, 2, 3, 13)
ONE_AT = (0, 3, 4, 17)
LAST_ONE, LAST_PAIR, LAST_CROSS = 21, 20, 21
BACK_AT = (0, 20, 21, 24)
OUT_AT = (22, 22, 22, 25)


def gradient_kernel(
    f_x, f_a, f_h, f_g, f_p, f_o, f_u, f_f, vec_in,
    total, vec_out,
    x, a, h, g, p, o, u, f,
    part, core_in, chain_pair, chain_one, y_in, end_in, vec, vec_got,
    load_sems, core_s, core_r, y_s, y_r, pair_s, pair_r, one_s, one_r, end_s, end_r,
    got, z_s, yy_s, kept, out_s, out_r, vec_s, vec_r,
):
    width = x.shape[1]
    slabs = g.shape[1] // width
    me = lax.axis_index("dp")
    core, y, z = me % 2, (me // 2) % 2, me // 4
    last = LANES_Z - 1
    core_peer, y_peer = {"dp": me + 1 - 2 * core}, {"dp": me + 2 - 4 * y}
    hop = [last - z, z]
    ahead = [{"dp": me - 4}, {"dp": me + 4}]
    behind = [ahead[1], ahead[0]]

    blocks = (
        [(a, 0, o, 0)]
        + [(x, 0, p, i) for i in range(3)]
        + [(h, 0, u, i) for i in range(slabs)]
        + [(g, i, f, 0) for i in range(slabs)]
    )
    duos = len(blocks) // 2
    sets = duos * SETS
    set_rows = width // SETS
    half = set_rows // 2
    piece = half // 4

    sources = [(f_a, a), (f_o, o), (f_x, x), (f_p, p), (f_h, h), (f_u, u), (f_f, f), (f_g, g)]
    loads = [
        pltpu.make_async_copy(src, dst, load_sems.at[i]) for i, (src, dst) in enumerate(sources)
    ]
    load_at = {0: (0, 1, 2, 3), 2 * SETS: (4, 5), (2 + slabs // 2) * SETS: (6, 7)}
    for load in loads[:4]:
        load.start()

    barrier = pltpu.get_barrier_semaphore()
    for peer in (core_peer, y_peer):
        pl.semaphore_signal(barrier, inc=1, device_id=peer, device_id_type=MESH)
    for d in range(2):
        @pl.when(hop[d] < last)
        def _():
            pl.semaphore_signal(barrier, inc=1, device_id=ahead[d], device_id_type=MESH)
    pl.semaphore_wait(barrier, jnp.where(jnp.logical_and(z > 0, z < last), 4, 3))

    def remote(src, dst, send, recv, peer):
        return pltpu.make_async_remote_copy(
            src_ref=src, dst_ref=dst, send_sem=send, recv_sem=recv,
            device_id=peer, device_id_type=MESH,
        )

    def span(k, d, first, count):
        start = (k % SETS) * set_rows + d * half + first * piece
        return pl.ds(pl.multiple_of(start, 16), count * piece)

    def mine(k, d, first, count=1):
        return part.at[k // SETS, core, span(k, d, first, count)]

    def final(k, d, first, count=1):
        return total.at[2 * (k // SETS) + core, span(k, d, first, count)]

    def add(dst, src):
        dst[...] = (dst[...].astype(F32) + src[...].astype(F32)).astype(BF16)

    def core_copy(k):
        rows = pl.ds(pl.multiple_of((k % SETS) * set_rows, set_rows), set_rows)
        return remote(
            part.at[k // SETS, 1 - core, rows], core_in.at[k], core_s.at[k], core_r.at[k], core_peer
        )

    def y_copy(k, d):
        return remote(mine(k, d, 1 - y), y_in.at[k, d], y_s.at[k, d], y_r.at[k, d], y_peer)

    def pair_copy(k, d):
        return remote(
            mine(k, d, 2, 2), chain_pair.at[k, d], pair_s.at[k, d], pair_r.at[k, d], ahead[d]
        )

    def one_copy(k, d):
        return remote(mine(k, d, y), chain_one.at[k, d], one_s.at[k, d], one_r.at[k, d], ahead[d])

    def end_copy(k, d):
        return remote(mine(k, d, 3 - y), end_in.at[k], end_s.at[k], end_r.at[k], y_peer)

    def spread_z(k, d, b, i, src):
        return remote(src, final(k, d, b), z_s.at[k, d, i], got.at[k, d, b], behind[d])

    def spread_y(k, d, b, i, src):
        return remote(src, final(k, d, b), yy_s.at[k, d, i], got.at[k, d, b], y_peer)

    def keep_copy(k, d, b, i):
        return pltpu.make_async_copy(mine(k, d, b), final(k, d, b), kept.at[k, d, i])

    def out_copy(k, d):
        return remote(
            final(k, d, 0, 4), final(k, d, 0, 4), out_s.at[k, d], out_r.at[k, d], core_peer
        )

    def arrived(k, d, b):
        spread_z(k, d, b, 0, final(k, d, b)).wait_recv()

    outer = jnp.logical_or(z == 0, z == last)
    z_pair = {"dp": me + 4 - 8 * (z % 2)}
    z_mid = {"dp": jnp.where(z == 1, me + 4, me - 4)}
    z_out = {"dp": jnp.where(z == 1, me - 4, me + 4)}

    def vec_copy(i, peer):
        return remote(vec.at[i], vec_got.at[min(i, 3)], vec_s.at[i], vec_r.at[min(i, 3)], peer)

    def compute(k):
        for i in load_at.get(k, ()):
            loads[i].wait()
        m, at = k // SETS, (k % SETS) * set_rows
        for side in range(2):
            left, i, right, j = blocks[2 * m + side]
            cols = slice(i * width + at, i * width + at + set_rows)
            part[m, side, at : at + set_rows, :] = dot_tn(
                left[:, cols], right[:, j * width : (j + 1) * width]
            ).astype(BF16)
        core_copy(k).start()

    vec[0] = vec_in[...]
    vec_copy(0, core_peer).start()
    compute(0)
    for load in loads[4:]:
        load.start()

    def feed(t):
        for k in range(1, sets):
            @pl.when(t == k - 1)
            def _():
                compute(k)

        for i, peer in ((1, y_peer), (2, z_pair)):
            @pl.when(t == i)
            def _():
                vec_copy(i - 1, peer).wait_recv()
                vec[i] = vec[i - 1] + vec_got[i - 1]
                vec_copy(i, peer).start()

        @pl.when(t == 3)
        def _():
            vec_copy(2, z_pair).wait_recv()
            vec[3] = vec[2] + vec_got[2]

            @pl.when(jnp.logical_not(outer))
            def _():
                vec_copy(3, z_mid).start()

        @pl.when(jnp.logical_and(t == 4, jnp.logical_not(outer)))
        def _():
            vec_copy(3, z_mid).wait_recv()
            vec[4] = vec[3] + vec_got[3]
            vec_copy(4, z_out).start()
            vec_out[...] = vec[4]

        @pl.when(jnp.logical_and(t == 5, outer))
        def _():
            vec_copy(3, z_mid).wait_recv()
            vec_out[...] = vec_got[3]

        @pl.when(t < sets)
        def _():
            core_copy(t).wait_recv()
            for d in range(2):
                add(mine(t, d, 0, 4), core_in.at[t, pl.ds(d * half, half)])
                y_copy(t, d).start()

                @pl.when(hop[d] == 0)
                def _():
                    pair_copy(t, d).start()

    def during(k, more=True):
        return jnp.logical_and(jnp.logical_and(k >= 0, k < sets), more)

    def by_place(place, offsets):
        out = jnp.int32(offsets[0])
        for i, offset in enumerate(offsets[1:], 1):
            out = jnp.where(place == i, offset, out)
        return out

    def arrive_y(t):
        k = t - ARRIVE_Y

        @pl.when(during(k))
        def _():
            for d in range(2):
                y_copy(k, d).wait_recv()
                add(mine(k, d, y), y_in.at[k, d])

                @pl.when(hop[d] == 0)
                def _():
                    one_copy(k, d).start()

    def hop_pair(t):
        for d in range(2):
            k = t - by_place(hop[d], PAIR_AT)

            @pl.when(during(k, hop[d] > 0))
            def _():
                pair_copy(k, d).wait_recv()
                add(mine(k, d, 2, 2), chain_pair.at[k, d])

                @pl.when(hop[d] < last)
                def _():
                    pair_copy(k, d).start()

                @pl.when(hop[d] == last)
                def _():
                    end_copy(k, d).start()

    def hop_one(t):
        for d in range(2):
            k = t - by_place(hop[d], ONE_AT)

            @pl.when(during(k, hop[d] > 0))
            def _():
                one_copy(k, d).wait_recv()
                add(mine(k, d, y), chain_one.at[k, d])

                @pl.when(hop[d] < last)
                def _():
                    one_copy(k, d).start()

    def last_one(t):
        k = t - LAST_ONE
        for d in range(2):
            @pl.when(during(k, hop[d] == last))
            def _():
                spread_z(k, d, y, 0, mine(k, d, y)).start()
                spread_y(k, d, y, 0, mine(k, d, y)).start()
                keep_copy(k, d, y, 0).start()

    def last_pair(t):
        k = t - LAST_PAIR
        for d in range(2):
            @pl.when(during(k, hop[d] == last))
            def _():
                end_copy(k, d).wait_recv()
                add(mine(k, d, 2 + y), end_in.at[k])
                spread_y(k, d, 2 + y, 1, mine(k, d, 2 + y)).start()
                spread_z(k, d, 2 + y, 1 + y, mine(k, d, 2 + y)).start()
                keep_copy(k, d, 2 + y, 1).start()

    def last_cross(t):
        k = t - LAST_CROSS
        for d in range(2):
            @pl.when(during(k, hop[d] == last))
            def _():
                arrived(k, d, 3 - y)
                spread_z(k, d, 3 - y, 2 - y, final(k, d, 3 - y)).start()

    def way_back(t):
        for d in range(2):
            k = t - by_place(last - hop[d], BACK_AT)

            @pl.when(during(k, hop[d] < last))
            def _():
                for i, b in ((0, y), (1, 2), (2, 3)):
                    arrived(k, d, b)

                    @pl.when(hop[d] > 0)
                    def _():
                        spread_z(k, d, b, i, final(k, d, b)).start()

                    if i == 0:
                        spread_y(k, d, b, 0, final(k, d, b)).start()

    def to_core(t):
        for d in range(2):
            k = t - by_place(last - hop[d], OUT_AT)

            @pl.when(during(k))
            def _():
                arrived(k, d, 1 - y)

                @pl.when(hop[d] == last)
                def _():
                    keep_copy(k, d, y, 0).wait()
                    keep_copy(k, d, 2 + y, 1).wait()

                out_copy(k, d).start()

    def tick(t, _):
        for stage in (
            last_one, hop_one, arrive_y, hop_pair, to_core, last_cross, feed, last_pair, way_back
        ):
            stage(t)
        return 0

    lax.fori_loop(0, sets + max(OUT_AT), tick, 0)

    def settle(k, _):
        core_copy(k).wait_send()
        for d in range(2):
            y_copy(k, d).wait_send()
            out_copy(k, d).wait()
            spread_y(k, d, y, 0, final(k, d, y)).wait_send()

            @pl.when(hop[d] < last)
            def _():
                pair_copy(k, d).wait_send()
                one_copy(k, d).wait_send()

            @pl.when(hop[d] == last)
            def _():
                end_copy(k, d).wait_send()
                spread_y(k, d, 2 + y, 1, final(k, d, 2 + y)).wait_send()

            @pl.when(hop[d] > 0)
            def _():
                for i, b in ((0, y), (1, 2), (2, 3)):
                    spread_z(k, d, b, i, final(k, d, b)).wait_send()

        return 0

    lax.fori_loop(0, sets, settle, 0)

    for i in range(3):
        vec_copy(i, core_peer).wait_send()

    @pl.when(jnp.logical_not(outer))
    def _():
        vec_copy(3, z_mid).wait_send()
        vec_copy(4, z_out).wait_send()


def reduce_gradients(factors, vectors):
    rows, width = factors[0].shape
    hidden = factors[3].shape[1]
    blocks = 4 + 2 * (hidden // width)
    duos = blocks // 2
    sets = duos * SETS
    piece = width // SETS // 8
    any_space = pl.BlockSpec(memory_space=pl.ANY)
    vmem = pl.BlockSpec(memory_space=pltpu.VMEM)
    low = lambda *shape: pltpu.VMEM(shape, BF16)
    dma = lambda *shape: pltpu.SemaphoreType.DMA(shape)
    return pl.pallas_call(
        gradient_kernel,
        out_shape=[
            jax.ShapeDtypeStruct((blocks, width, width), BF16),
            jax.ShapeDtypeStruct(vectors.shape, F32),
        ],
        in_specs=[any_space] * 8 + [vmem],
        out_specs=[any_space, vmem],
        scratch_shapes=[low(*factor.shape) for factor in factors]
        + [
            low(duos, 2, width, width), low(sets, width // SETS, width),
            low(sets, 2, 2 * piece, width), low(sets, 2, piece, width),
            low(sets, 2, piece, width), low(sets, piece, width),
            pltpu.VMEM((5,) + vectors.shape, F32), pltpu.VMEM((4,) + vectors.shape, F32),
            dma(8), dma(sets), dma(sets), dma(sets, 2), dma(sets, 2), dma(sets, 2), dma(sets, 2),
            dma(sets, 2), dma(sets, 2), dma(sets), dma(sets),
            dma(sets, 2, 4), dma(sets, 2, 3), dma(sets, 2, 2), dma(sets, 2, 2), dma(sets, 2),
            dma(sets, 2), dma(5), dma(4),
        ],
        compiler_params=pltpu.CompilerParams(
            collective_id=1, has_side_effects=True, vmem_limit_bytes=VMEM_BYTES
        ),
        name="gradients",
    )(*factors, vectors)


def widen_kernel(slabs, total, vec, low_results, *refs):
    outs, results = refs[:12], refs[12]
    low, high, held, in_sems, out_sems, side_sems = refs[13:]
    blocks, width, _ = total.shape
    inward, outward, expand, shrink = outs[:4]

    def reads(i):
        return pltpu.make_async_copy(total.at[i], low.at[i], in_sems.at[i])

    def place(i):
        if i < 1:
            return outward
        if i < 4:
            return inward.at[:, pl.ds((i - 1) * width, width)]
        if i < 4 + slabs:
            return expand.at[:, pl.ds((i - 4) * width, width)]
        return shrink.at[pl.ds((i - 4 - slabs) * width, width)]

    def writes(i):
        return pltpu.make_async_copy(high.at[i], place(i), out_sems.at[i])

    side_in = pltpu.make_async_copy(low_results, held, side_sems.at[0])
    side_out = pltpu.make_async_copy(held, results, side_sems.at[1])
    for i in range(blocks):
        reads(i).start()
    side_in.start()
    row = 0
    for out in outs[4:]:
        for i in range(out.shape[1] // width):
            out[:, i * width : (i + 1) * width] = vec[row : row + 1, :]
            row += 1
    for i in range(blocks):
        reads(i).wait()

        def part(r, _):
            rows = pl.ds(pl.multiple_of(r * 64, 64), 64)
            high[i, rows] = low[i, rows].astype(F32)
            return 0

        lax.fori_loop(0, width // 64, part, 0)
        writes(i).start()
    side_in.wait()
    side_out.start()
    for i in range(blocks):
        writes(i).wait()
    side_out.wait()


def widen(total, vec, low_results, hidden):
    blocks, width, _ = total.shape
    slabs = hidden // width
    shapes = [(width, 3 * width), (width, width), (width, hidden), (hidden, width)]
    lengths = [3 * width, width, width, width, hidden, width, width, width]
    any_space = pl.BlockSpec(memory_space=pl.ANY)
    vmem = pl.BlockSpec(memory_space=pltpu.VMEM)
    dma = lambda *shape: pltpu.SemaphoreType.DMA(shape)
    return pl.pallas_call(
        partial(widen_kernel, slabs),
        out_shape=[jax.ShapeDtypeStruct(shape, F32) for shape in shapes]
        + [jax.ShapeDtypeStruct((1, n), F32) for n in lengths]
        + [jax.ShapeDtypeStruct(low_results.shape, BF16)],
        in_specs=[any_space, vmem, any_space],
        out_specs=[any_space] * 4 + [vmem] * 8 + [any_space],
        scratch_shapes=[
            pltpu.VMEM((blocks, width, width), BF16), pltpu.VMEM((blocks, width, width), F32),
            pltpu.VMEM(low_results.shape, BF16), dma(blocks), dma(blocks), dma(2),
        ],
        compiler_params=pltpu.CompilerParams(vmem_limit_bytes=VMEM_BYTES),
        name="widen",
    )(total, vec, low_results)


def shards(
    boundary, inward, inbias, outward, outbias, normgain, normshift, expand, expbias,
    shrink, shrbias, lastgain, lastshift,
):
    width = outward.shape[-1]
    hidden = expand.shape[-1]
    slabs = hidden // width
    outs = run_layer(
        boundary[0],
        (inward[0], outward[0], expand[0], shrink[0]),
        (inbias, outbias, normgain, normshift, expbias, shrbias, lastgain, lastshift),
    )
    results, factors, vectors = outs[0], outs[1:9], outs[9]
    if lax.axis_size("dp") == 4 * LANES_Z:
        total, vec = reduce_gradients(factors, vectors)
        widened = widen(total, vec, results, hidden)
        matrices, pieces, results = widened[:4], widened[4:12], widened[12]
    else:
        f_x, f_a, f_h, f_g, f_p, f_o, f_u, f_f = factors

        def summed(left, right):
            grad = dot_tn(left, right).astype(BF16)
            mine = lax.psum_scatter(grad, "dp", scatter_dimension=0, tiled=True)
            return lax.all_gather(mine, "dp", axis=0, tiled=True).astype(F32)

        matrices = [summed(f_x, f_p), summed(f_a, f_o), summed(f_h, f_u), summed(f_g, f_f)]
        vec = lax.psum(vectors, "dp")
        pieces, row = [], 0
        for count in (3, 1, 1, 1, slabs, 1, 1, 1):
            pieces.append(vec[row : row + count].reshape(1, count * width))
            row += count

    inward_grad, outward_grad, expand_grad, shrink_grad = (m[None] for m in matrices)
    return (
        results[None],
        inward_grad, pieces[0], outward_grad, pieces[1], pieces[2], pieces[3],
        expand_grad, pieces[4], shrink_grad, pieces[5], pieces[6], pieces[7],
    )


def solution(mesh):
    matrix, vector = P("section", None, None), P("section", None)
    params = (
        matrix, vector, matrix, vector, vector, vector, matrix, vector, matrix, vector,
        vector, vector,
    )
    specs = (P("section", "dp", None),) + params
    return jax.shard_map(shards, mesh=mesh, in_specs=specs, out_specs=specs, check_vma=False)
```

profile of v0, /device:TPU:0, one launch (start us, length us, event | category | flops | bytes accessed | tf_op | source)
XLA Modules:
  0.0 285.4 jit_solution(4689999024560008367)
XLA Ops:
  0.6 113.9 %layer.1 = (bf16[1024,768]{1,0:T(8,128)(2,1)}, bf16[1024,768]{1,0:T(8,128)(2,1)}, bf16[1024,768]{1,0:T(8,128)(2,1)}, bf16[1024,768]{1,0:T(8,128)(2,1)}, bf16[102...) custom-call(bf16[1024,768]{1,0:T(8,128)(2,1)} %bitcast.13, ...), custom_call_target="tpu_custom_call" | custom-call | tf_op jit(solution)/shard_map/layer/pallas_call | solution.py:403
  114.5 154.7 %gradients.1 = (bf16[12,768,768]{2,1,0:T(8,128)(2,1)}, f32[16,768]{1,0:T(8,128)}) custom-call(bf16[1024,768]{1,0:T(8,128)(2,1)} %get-tuple-element.38.f_x, bf16[1024,768]{1,0:T(8,128)(2,1)} %get-tuple-element.39.f_a, bf16[1024,768]{1,0:T(8,128)(2,1)} %get-tuple-element.40.f_h, bf16[1024,3072]{1,0:T(8,128)(2,1)} %get-tuple-element.41.f_g, ...), custom_call_target="tpu_custom_call" | custom-call | tf_op jit(solution)/shard_map/gradients/pallas_call | solution.py:777
  269.2 16.0 %widen.1 = (f32[768,2304]{1,0:T(8,128)}, f32[768,768]{1,0:T(8,128)}, f32[768,3072]{1,0:T(8,128)}, f32[3072,768]{1,0:T(8,128)}, f32[1,2304]{1,0:T(1,128)}, /*inde...) custom-call(bf16[12,768,768]{2,1,0:T(8,128)(2,1)} %get-tuple-element, ...), custom_call_target="tpu_custom_call" | custom-call | tf_op jit(solution)/shard_map/widen/pallas_call | solution.py:859
where the time goes:
time: 286 us; the launch traced here: 285 us
  Pallas kernels  285 us (100%)
    pallas_call x1, Pallas kernels, reduce_gradients(): pl.pallas_call(gradient_kernel, out_shape=[jax.ShapeDtypeStruct((blocks,...  155 us
    pallas_call x1, Pallas kernels, run_layer(): pl.pallas_call(layer_kernel, out_shape=out_shape, in_specs=[any_space] *...  114 us
    pallas_call x1, Pallas kernels, widen(): pl.pallas_call(partial(widen_kernel, slabs), out_shape=[jax.ShapeDtypeStr...  16 us

commit v1 on v0

--- a/solution.py
+++ b/solution.py
@@ -18,6 +18,9 @@
 F32 = jnp.float32
 BF16 = jnp.bfloat16
 VMEM_BYTES = 63 * 2**20
+LAYER_VMEM = 63 * 2**20
+GRADIENT_VMEM = 46 * 2**20
+WIDEN_VMEM = 34 * 2**20
 
 
 def dot(a, b):
@@ -61,7 +64,7 @@
     near, far, masks,
     results, f_x, f_a, f_h, f_g, f_p, f_o, f_u, f_f, vector_rows,
     win, wout, wexp, wshr,
-    xs, qkv, att, low, zin, hbs, gs, gps, n1s, n2s, s1s, s2s, dys, ybuf, xbuf,
+    xs, qkv, att, low, zin, hbs, gs, gps, n1s, n2s, scales, dys, ybuf,
     acc, keep, das, carry, vectors,
     load_sems, out_sems, res_sems, fwd_send, fwd_recv, bwd_send, bwd_recv,
 ):
@@ -110,15 +113,15 @@
 
     def send_backward(c):
         return pltpu.make_async_remote_copy(
-            src_ref=xbuf.at[rows_of(c)], dst_ref=dys.at[rows_of(c)],
+            src_ref=ybuf.at[rows_of(c)], dst_ref=dys.at[rows_of(c)],
             send_sem=bwd_send.at[c], recv_sem=bwd_recv.at[c],
             device_id=peer, device_id_type=MESH,
         )
 
-    def result_copy(buf, c):
-        return pltpu.make_async_copy(buf.at[rows_of(c)], results.at[rows_of(c)], res_sems.at[c])
-
-    early = [(xs, f_x), (att, f_a), (hbs, f_h), (gs, f_g)]
+    def result_copy(c):
+        return pltpu.make_async_copy(ybuf.at[rows_of(c)], results.at[rows_of(c)], res_sems.at[c])
+
+    early = [(xs, f_x), (att, f_a), (hbs, f_h)]
     late = [(qkv, f_p), (n1s, f_o), (gps, f_u), (n2s, f_f)]
 
     def factor_copies(c, which, base):
@@ -126,6 +129,9 @@
             pltpu.make_async_copy(src.at[rows_of(c)], dst.at[rows_of(c)], out_sems.at[c, base + i])
             for i, (src, dst) in enumerate(which)
         ]
+
+    def active_copy(c):
+        return pltpu.make_async_copy(gs.at[c % 2], f_g.at[rows_of(c)], out_sems.at[c, 3])
 
     def column_sum(at, value):
         vectors[at] += jnp.sum(value, axis=0, keepdims=True)
@@ -253,23 +259,28 @@
         e = xs[rows, :].astype(F32) + (dot(att[rows, :], wout[...]) + outbias[...])
         n1, s1 = norm_forward(e)
         n1s[rows, :] = n1.astype(BF16)
-        s1s[rows, :] = s1
+        scales[rows, 0:1] = s1
         h = n1 * normgain[...] + normshift[...]
         hbs[rows, :] = h.astype(BF16)
+
+        @pl.when(c >= 2)
+        def _():
+            active_copy(c - 2).wait()
+
         acc[...] = h + shrbias[...]
         for i in range(slabs):
             cols = slice(i * width, (i + 1) * width)
             u = dot(hbs[rows, :], wexp[:, cols]) + expbias[:, cols]
             phi = 0.5 * (1.0 + lax.erf(u * math.sqrt(0.5)))
             g = (u * phi).astype(BF16)
-            gs[rows, cols] = g
+            gs[c % 2, :, cols] = g
             gps[rows, cols] = (
                 phi + u * (jnp.exp(u * u * -0.5) * (1.0 / math.sqrt(2.0 * math.pi)))
             ).astype(BF16)
             acc[...] += dot(g, wshr[cols, :])
         n2, s2 = norm_forward(acc[...])
         n2s[rows, :] = n2.astype(BF16)
-        s2s[rows, :] = s2
+        scales[rows, 1:2] = s2
         ybuf[rows, :] = (n2 * lastgain[...] + lastshift[...]).astype(BF16)
 
         @pl.when(first)
@@ -278,9 +289,9 @@
 
         @pl.when(jnp.logical_not(first))
         def _():
-            result_copy(ybuf, c).start()
-
-        for copy in factor_copies(c, early, 0):
+            result_copy(c).start()
+
+        for copy in factor_copies(c, early, 0) + [active_copy(c)]:
             copy.start()
 
     def backward(c):
@@ -298,7 +309,7 @@
         n2 = n2s[rows, :].astype(F32)
         column_sum(7 + slabs, dy * n2)
         column_sum(8 + slabs, dy)
-        dr = norm_backward(dy * lastgain[...], n2, s2s[rows, :])
+        dr = norm_backward(dy * lastgain[...], n2, scales[rows, 1:2])
         df = dr.astype(BF16)
         n2s[rows, :] = df
         column_sum(6 + slabs, df.astype(F32))
@@ -314,7 +325,7 @@
         n1 = n1s[rows, :].astype(F32)
         column_sum(4, dh * n1)
         column_sum(5, dh)
-        de = norm_backward(dh * normgain[...], n1, s1s[rows, :])
+        de = norm_backward(dh * normgain[...], n1, scales[rows, 0:1])
         keep[...] = de
         do = de.astype(BF16)
         n1s[rows, :] = do
@@ -332,11 +343,20 @@
         for i in range(3):
             column_sum(i, qkv[rows, i * width : (i + 1) * width].astype(F32))
         dx = keep[...] + dot_nt(qkv[rows, :], win[...])
-        xbuf[rows, :] = dx.astype(BF16)
 
         @pl.when(first)
         def _():
-            result_copy(xbuf, c).start()
+            send_forward(c).wait_send()
+
+        @pl.when(jnp.logical_not(first))
+        def _():
+            result_copy(c).wait()
+
+        ybuf[rows, :] = dx.astype(BF16)
+
+        @pl.when(first)
+        def _():
+            result_copy(c).start()
 
         @pl.when(jnp.logical_not(first))
         def _():
@@ -369,16 +389,19 @@
     def finish(c, _):
         @pl.when(first)
         def _():
-            send_forward(c).wait_send()
-            result_copy(xbuf, c).wait()
+            result_copy(c).wait()
 
         @pl.when(jnp.logical_not(first))
         def _():
             send_backward(c).wait_send()
-            result_copy(ybuf, c).wait()
 
         for copy in factor_copies(c, early, 0) + factor_copies(c, late, 4):
             copy.wait()
+
+        @pl.when(c >= chunks - 2)
+        def _():
+            active_copy(c).wait()
+
         return 0
 
     lax.fori_loop(0, chunks, finish, 0)
@@ -408,16 +431,16 @@
         scratch_shapes=[
             low(width, 3 * width), low(width, width), low(width, hidden), low(hidden, width),
             low(rows, width), low(rows, 3 * width), low(rows, width), low(rows, width),
-            low(rows, width), low(rows, width), low(rows, hidden), low(rows, hidden),
-            low(rows, width), low(rows, width), wide(rows, 1), wide(rows, 1),
-            low(rows, width), low(rows, width), low(rows, width),
+            low(rows, width), low(rows, width), low(2, CHUNK, hidden), low(rows, hidden),
+            low(rows, width), low(rows, width), wide(rows, 2),
+            low(rows, width), low(rows, width),
             wide(CHUNK, width), wide(CHUNK, width), low(CHUNK, width), wide(CHUNK, 2 * width),
             wide(vector_count, 1, width),
             dma((5,)), dma((chunks, 8)), dma((chunks,)), dma((chunks,)), dma((chunks,)),
             dma((chunks,)), dma((chunks,)),
         ],
         compiler_params=pltpu.CompilerParams(
-            collective_id=0, has_side_effects=True, vmem_limit_bytes=VMEM_BYTES
+            collective_id=0, has_side_effects=True, vmem_limit_bytes=LAYER_VMEM
         ),
         name="layer",
     )(boundary, *weights, *biases, jnp.asarray(near), jnp.asarray(far), jnp.asarray(masks))
@@ -425,6 +448,7 @@
 
 SETS = 2
 LANES_Z = 4
+STAGES = 3
 
 ARRIVE_Y = 2
 PAIR_AT = (0, 2, 3, 13)
@@ -438,9 +462,9 @@
     f_x, f_a, f_h, f_g, f_p, f_o, f_u, f_f, vec_in,
     total, vec_out,
     x, a, h, g, p, o, u, f,
-    part, core_in, chain_pair, chain_one, y_in, end_in, vec, vec_got,
+    own, stage, core_in, chain_pair, chain_one, y_in, end_in, vec, vec_got,
     load_sems, core_s, core_r, y_s, y_r, pair_s, pair_r, one_s, one_r, end_s, end_r,
-    got, z_s, yy_s, kept, out_s, out_r, vec_s, vec_r,
+    got, z_s, yy_s, kept, out_s, out_r, vec_s, vec_r, credit,
 ):
     width = x.shape[1]
     slabs = g.shape[1] // width
@@ -492,7 +516,8 @@
         return pl.ds(pl.multiple_of(start, 16), count * piece)
 
     def mine(k, d, first, count=1):
-        return part.at[k // SETS, core, span(k, d, first, count)]
+        return own.at[k // SETS, span(k, d, first, count)]
+
 
     def final(k, d, first, count=1):
         return total.at[2 * (k // SETS) + core, span(k, d, first, count)]
@@ -501,9 +526,9 @@
         dst[...] = (dst[...].astype(F32) + src[...].astype(F32)).astype(BF16)
 
     def core_copy(k):
-        rows = pl.ds(pl.multiple_of((k % SETS) * set_rows, set_rows), set_rows)
         return remote(
-            part.at[k // SETS, 1 - core, rows], core_in.at[k], core_s.at[k], core_r.at[k], core_peer
+            stage.at[k % STAGES, 1 - core], core_in.at[k % STAGES], core_s.at[k], core_r.at[k],
+            core_peer,
         )
 
     def y_copy(k, d):
@@ -548,11 +573,14 @@
     def compute(k):
         for i in load_at.get(k, ()):
             loads[i].wait()
+        if k >= STAGES:
+            core_copy(k - STAGES).wait_send()
+            pl.semaphore_wait(credit, 1)
         m, at = k // SETS, (k % SETS) * set_rows
         for side in range(2):
             left, i, right, j = blocks[2 * m + side]
             cols = slice(i * width + at, i * width + at + set_rows)
-            part[m, side, at : at + set_rows, :] = dot_tn(
+            stage[k % STAGES, side] = dot_tn(
                 left[:, cols], right[:, j * width : (j + 1) * width]
             ).astype(BF16)
         core_copy(k).start()
@@ -601,12 +629,18 @@
         def _():
             core_copy(t).wait_recv()
             for d in range(2):
-                add(mine(t, d, 0, 4), core_in.at[t, pl.ds(d * half, half)])
+                here = stage[t % STAGES, core, d * half : (d + 1) * half].astype(F32)
+                there = core_in[t % STAGES, d * half : (d + 1) * half].astype(F32)
+                mine(t, d, 0, 4)[...] = (here + there).astype(BF16)
                 y_copy(t, d).start()
 
                 @pl.when(hop[d] == 0)
                 def _():
                     pair_copy(t, d).start()
+
+            @pl.when(t < sets - STAGES)
+            def _():
+                pl.semaphore_signal(credit, inc=1, device_id=core_peer, device_id_type=MESH)
 
     def during(k, more=True):
         return jnp.logical_and(jnp.logical_and(k >= 0, k < sets), more)
@@ -729,7 +763,6 @@
     lax.fori_loop(0, sets + max(OUT_AT), tick, 0)
 
     def settle(k, _):
-        core_copy(k).wait_send()
         for d in range(2):
             y_copy(k, d).wait_send()
             out_copy(k, d).wait()
@@ -753,6 +786,8 @@
         return 0
 
     lax.fori_loop(0, sets, settle, 0)
+    for k in range(sets - STAGES, sets):
+        core_copy(k).wait_send()
 
     for i in range(3):
         vec_copy(i, core_peer).wait_send()
@@ -770,31 +805,29 @@
     duos = blocks // 2
     sets = duos * SETS
     piece = width // SETS // 8
-    any_space = pl.BlockSpec(memory_space=pl.ANY)
     vmem = pl.BlockSpec(memory_space=pltpu.VMEM)
     low = lambda *shape: pltpu.VMEM(shape, BF16)
     dma = lambda *shape: pltpu.SemaphoreType.DMA(shape)
+    any_space = pl.BlockSpec(memory_space=pl.ANY)
     return pl.pallas_call(
         gradient_kernel,
-        out_shape=[
-            jax.ShapeDtypeStruct((blocks, width, width), BF16),
-            jax.ShapeDtypeStruct(vectors.shape, F32),
-        ],
+        out_shape=[low(blocks, width, width), jax.ShapeDtypeStruct(vectors.shape, F32)],
         in_specs=[any_space] * 8 + [vmem],
-        out_specs=[any_space, vmem],
+        out_specs=[vmem, vmem],
         scratch_shapes=[low(*factor.shape) for factor in factors]
         + [
-            low(duos, 2, width, width), low(sets, width // SETS, width),
+            low(duos, width, width), low(STAGES, 2, width // SETS, width),
+            low(STAGES, width // SETS, width),
             low(sets, 2, 2 * piece, width), low(sets, 2, piece, width),
             low(sets, 2, piece, width), low(sets, piece, width),
             pltpu.VMEM((5,) + vectors.shape, F32), pltpu.VMEM((4,) + vectors.shape, F32),
             dma(8), dma(sets), dma(sets), dma(sets, 2), dma(sets, 2), dma(sets, 2), dma(sets, 2),
             dma(sets, 2), dma(sets, 2), dma(sets), dma(sets),
             dma(sets, 2, 4), dma(sets, 2, 3), dma(sets, 2, 2), dma(sets, 2, 2), dma(sets, 2),
-            dma(sets, 2), dma(5), dma(4),
+            dma(sets, 2), dma(5), dma(4), pltpu.SemaphoreType.REGULAR,
         ],
         compiler_params=pltpu.CompilerParams(
-            collective_id=1, has_side_effects=True, vmem_limit_bytes=VMEM_BYTES
+            collective_id=1, has_side_effects=True, vmem_limit_bytes=GRADIENT_VMEM
         ),
         name="gradients",
     )(*factors, vectors)
@@ -802,12 +835,9 @@
 
 def widen_kernel(slabs, total, vec, low_results, *refs):
     outs, results = refs[:12], refs[12]
-    low, high, held, in_sems, out_sems, side_sems = refs[13:]
+    high, held, out_sems, side_sems = refs[13:]
     blocks, width, _ = total.shape
     inward, outward, expand, shrink = outs[:4]
-
-    def reads(i):
-        return pltpu.make_async_copy(total.at[i], low.at[i], in_sems.at[i])
 
     def place(i):
         if i < 1:
@@ -823,8 +853,6 @@
 
     side_in = pltpu.make_async_copy(low_results, held, side_sems.at[0])
     side_out = pltpu.make_async_copy(held, results, side_sems.at[1])
-    for i in range(blocks):
-        reads(i).start()
     side_in.start()
     row = 0
     for out in outs[4:]:
@@ -832,11 +860,9 @@
             out[:, i * width : (i + 1) * width] = vec[row : row + 1, :]
             row += 1
     for i in range(blocks):
-        reads(i).wait()
-
         def part(r, _):
             rows = pl.ds(pl.multiple_of(r * 64, 64), 64)
-            high[i, rows] = low[i, rows].astype(F32)
+            high[i, rows] = total[i, rows].astype(F32)
             return 0
 
         lax.fori_loop(0, width // 64, part, 0)
@@ -861,15 +887,15 @@
         out_shape=[jax.ShapeDtypeStruct(shape, F32) for shape in shapes]
         + [jax.ShapeDtypeStruct((1, n), F32) for n in lengths]
         + [jax.ShapeDtypeStruct(low_results.shape, BF16)],
-        in_specs=[any_space, vmem, any_space],
+        in_specs=[vmem, vmem, any_space],
         out_specs=[any_space] * 4 + [vmem] * 8 + [any_space],
         scratch_shapes=[
-            pltpu.VMEM((blocks, width, width), BF16), pltpu.VMEM((blocks, width, width), F32),
-            pltpu.VMEM(low_results.shape, BF16), dma(blocks), dma(blocks), dma(2),
+            pltpu.VMEM((blocks, width, width), F32), pltpu.VMEM(low_results.shape, BF16),
+            dma(blocks), dma(2),
         ],
-        compiler_params=pltpu.CompilerParams(vmem_limit_bytes=VMEM_BYTES),
+        compiler_params=pltpu.CompilerParams(vmem_limit_bytes=WIDEN_VMEM),
         name="widen",
-    )(total, vec, low_results)
+    )(pltpu.with_memory_space_constraint(total, pltpu.VMEM), vec, low_results)
 
 
 def shards(

time: 286 us -> 278 us (0.972)
  Pallas kernels: 285 us -> 276 us
    pallas_call x1, Pallas kernels: 16 us -> 10.9 us  [widen(): pl.pallas_call(partial(widen_kernel, slabs), out_shape=[jax.ShapeDtypeStr...]
    pallas_call x1, Pallas kernels: 155 us -> 151 us  [reduce_gradients(): pl.pallas_call(gradient_kernel, out_shape=[low(blocks, width, width), jax...]
where the time goes in v1:
time: 278 us
  Pallas kernels  276 us (99%)
    pallas_call x1, Pallas kernels, reduce_gradients(): pl.pallas_call(gradient_kernel, out_shape=[low(blocks, width, width), jax...  151 us
    pallas_call x1, Pallas kernels, run_layer(): pl.pallas_call(layer_kernel, out_shape=out_shape, in_specs=[any_space] *...  114 us
    pallas_call x1, Pallas kernels, widen(): pl.pallas_call(partial(widen_kernel, slabs), out_shape=[jax.ShapeDtypeStr...  10.9 us

profile of v1, /device:TPU:0, one launch (start us, length us, event | category | flops | bytes accessed | tf_op | source)
XLA Modules:
  0.0 278.0 jit_solution(14619200159681732197)
XLA Ops:
  0.6 114.3 %layer.1 = (bf16[1024,768]{1,0:T(8,128)(2,1)}, bf16[1024,768]{1,0:T(8,128)(2,1)}, bf16[1024,768]{1,0:T(8,128)(2,1)}, bf16[1024,768]{1,0:T(8,128)(2,1)}, bf16[102...) custom-call(bf16[1024,768]{1,0:T(8,128)(2,1)} %bitcast.13, ...), custom_call_target="tpu_custom_call" | custom-call | tf_op jit(solution)/shard_map/layer/pallas_call | solution.py:426
  114.9 0.0 copy-start
  114.9 151.2 %gradients.1 = (bf16[12,768,768]{2,1,0:T(8,128)(2,1)S(1)}, f32[16,768]{1,0:T(8,128)}) custom-call(bf16[1024,768]{1,0:T(8,128)(2,1)} %get-tuple-element.38.f_x, bf16[1024,768]{1,0:T(8,128)(2,1)} %get-tuple-element.39.f_a, bf16[1024,768]{1,0:T(8,128)(2,1)} %get-tuple-element.40.f_h, bf16[1024,3072]{1,0:T(8,128)(2,1)} %get-tuple-element.41.f_g, ...), custom_call_target="tpu_custom_call" | custom-call | tf_op jit(solution)/shard_map/gradients/pallas_call | solution.py:812
  266.1 0.0 copy-done
  266.2 0.0 copy-start.1
  266.2 0.8 copy-done.1
  267.0 10.9 %widen.1 = (f32[768,2304]{1,0:T(8,128)}, f32[768,768]{1,0:T(8,128)}, f32[768,3072]{1,0:T(8,128)}, f32[3072,768]{1,0:T(8,128)}, f32[1,2304]{1,0:T(1,128)}, /*inde...) custom-call(bf16[12,768,768]{2,1,0:T(8,128)(2,1)S(1)} %get-tuple-ele, ...), custom_call_target="tpu_custom_call" | custom-call | tf_op jit(solution)/shard_map/widen/pallas_call | solution.py:885
Async XLA Ops:
  114.9 151.2 %copy-start = (bf16[1024,768]{1,0:T(8,128)(2,1)S(1)}, bf16[1024,768]{1,0:T(8,128)(2,1)}, u32[]{:S(2)}) copy-start(bf16[1024,768]{1,0:T(8,128)(2,1)} %get-tuple-element.49.low_results) | copy-start | bytes 4718596
  266.2 0.8 copy-start.1

commit v2 on v1

--- a/solution.py
+++ b/solution.py
@@ -83,14 +83,16 @@
             [(inward, win), (outward, wout), (expand, wexp), (shrink, wshr)]
         )
     ]
-    load_x = pltpu.make_async_copy(boundary, xs, load_sems.at[4])
+    head, rest = pl.ds(0, CHUNK), pl.ds(CHUNK, rows_all - CHUNK)
+    load_x = pltpu.make_async_copy(boundary.at[head], xs.at[head], load_sems.at[4])
+    load_rest = pltpu.make_async_copy(boundary.at[rest], xs.at[rest], load_sems.at[5])
     load_y = pltpu.make_async_copy(boundary, dys, load_sems.at[4])
-
-    loads[0].start()
 
     @pl.when(first)
     def _():
         load_x.start()
+
+    loads[0].start()
 
     @pl.when(jnp.logical_not(first))
     def _():
@@ -234,6 +236,10 @@
             for load in loads[1:]:
                 load.start()
 
+            @pl.when(first)
+            def _():
+                load_rest.start()
+
         @pl.when(jnp.logical_not(first))
         def _():
             send_forward(c).wait_recv()
@@ -255,6 +261,10 @@
         def _():
             for load in loads[1:]:
                 load.wait()
+
+            @pl.when(first)
+            def _():
+                load_rest.wait()
 
         e = xs[rows, :].astype(F32) + (dot(att[rows, :], wout[...]) + outbias[...])
         n1, s1 = norm_forward(e)
@@ -436,7 +446,7 @@
             low(rows, width), low(rows, width),
             wide(CHUNK, width), wide(CHUNK, width), low(CHUNK, width), wide(CHUNK, 2 * width),
             wide(vector_count, 1, width),
-            dma((5,)), dma((chunks, 8)), dma((chunks,)), dma((chunks,)), dma((chunks,)),
+            dma((6,)), dma((chunks, 8)), dma((chunks,)), dma((chunks,)), dma((chunks,)),
             dma((chunks,)), dma((chunks,)),
         ],
         compiler_params=pltpu.CompilerParams(
@@ -488,11 +498,14 @@
     half = set_rows // 2
     piece = half // 4
 
-    sources = [(f_a, a), (f_o, o), (f_x, x), (f_p, p), (f_h, h), (f_u, u), (f_f, f), (f_g, g)]
+    slabs_p = [pl.ds(i * width, width) for i in range(3)]
+    sources = [(f_a, a), (f_o, o), (f_x, x)]
+    sources += [(f_p.at[:, cols], p.at[:, cols]) for cols in slabs_p]
+    sources += [(f_h, h), (f_u, u), (f_f, f), (f_g, g)]
     loads = [
         pltpu.make_async_copy(src, dst, load_sems.at[i]) for i, (src, dst) in enumerate(sources)
     ]
-    load_at = {0: (0, 1, 2, 3), 2 * SETS: (4, 5), (2 + slabs // 2) * SETS: (6, 7)}
+    load_at = {0: (0, 1, 2, 3), SETS: (4, 5), 2 * SETS: (6, 7), (2 + slabs // 2) * SETS: (8, 9)}
     for load in loads[:4]:
         load.start()
 
@@ -821,7 +834,7 @@
             low(sets, 2, 2 * piece, width), low(sets, 2, piece, width),
             low(sets, 2, piece, width), low(sets, piece, width),
             pltpu.VMEM((5,) + vectors.shape, F32), pltpu.VMEM((4,) + vectors.shape, F32),
-            dma(8), dma(sets), dma(sets), dma(sets, 2), dma(sets, 2), dma(sets, 2), dma(sets, 2),
+            dma(10), dma(sets), dma(sets), dma(sets, 2), dma(sets, 2), dma(sets, 2), dma(sets, 2),
             dma(sets, 2), dma(sets, 2), dma(sets), dma(sets),
             dma(sets, 2, 4), dma(sets, 2, 3), dma(sets, 2, 2), dma(sets, 2, 2), dma(sets, 2),
             dma(sets, 2), dma(5), dma(4), pltpu.SemaphoreType.REGULAR,

time: 278 us -> 277 us (level)
  no operation moved by 1% of the time
where the time goes in v2:
time: 277 us
  Pallas kernels  275 us (99%)
    pallas_call x1, Pallas kernels, reduce_gradients(): pl.pallas_call(gradient_kernel, out_shape=[low(blocks, width, width), jax...  150 us
    pallas_call x1, Pallas kernels, run_layer(): pl.pallas_call(layer_kernel, out_shape=out_shape, in_specs=[any_space] *...  114 us
    pallas_call x1, Pallas kernels, widen(): pl.pallas_call(partial(widen_kernel, slabs), out_shape=[jax.ShapeDtypeStr...  10.9 us

profile of v2, /device:TPU:0, one launch (start us, length us, event | category | flops | bytes accessed | tf_op | source)
XLA Modules:
  0.0 276.8 jit_solution(2855743710805862002)
XLA Ops:
  0.6 114.2 %layer.1 = (bf16[1024,768]{1,0:T(8,128)(2,1)}, bf16[1024,768]{1,0:T(8,128)(2,1)}, bf16[1024,768]{1,0:T(8,128)(2,1)}, bf16[1024,768]{1,0:T(8,128)(2,1)}, bf16[102...) custom-call(bf16[1024,768]{1,0:T(8,128)(2,1)} %bitcast.13, ...), custom_call_target="tpu_custom_call" | custom-call | tf_op jit(solution)/shard_map/layer/pallas_call | solution.py:436
  114.9 0.0 copy-start
  114.9 150.1 %gradients.1 = (bf16[12,768,768]{2,1,0:T(8,128)(2,1)S(1)}, f32[16,768]{1,0:T(8,128)}) custom-call(bf16[1024,768]{1,0:T(8,128)(2,1)} %get-tuple-element.38.f_x, bf16[1024,768]{1,0:T(8,128)(2,1)} %get-tuple-element.39.f_a, bf16[1024,768]{1,0:T(8,128)(2,1)} %get-tuple-element.40.f_h, bf16[1024,3072]{1,0:T(8,128)(2,1)} %get-tuple-element.41.f_g, ...), custom_call_target="tpu_custom_call" | custom-call | tf_op jit(solution)/shard_map/gradients/pallas_call | solution.py:825
  265.0 0.0 copy-done
  265.0 0.0 copy-start.1
  265.0 0.8 copy-done.1
  265.8 10.9 %widen.1 = (f32[768,2304]{1,0:T(8,128)}, f32[768,768]{1,0:T(8,128)}, f32[768,3072]{1,0:T(8,128)}, f32[3072,768]{1,0:T(8,128)}, f32[1,2304]{1,0:T(1,128)}, /*inde...) custom-call(bf16[12,768,768]{2,1,0:T(8,128)(2,1)S(1)} %get-tuple-ele, ...), custom_call_target="tpu_custom_call" | custom-call | tf_op jit(solution)/shard_map/widen/pallas_call | solution.py:898
Async XLA Ops:
  114.9 150.1 %copy-start = (bf16[1024,768]{1,0:T(8,128)(2,1)S(1)}, bf16[1024,768]{1,0:T(8,128)(2,1)}, u32[]{:S(2)}) copy-start(bf16[1024,768]{1,0:T(8,128)(2,1)} %get-tuple-element.49.low_results) | copy-start | bytes 4718596
  265.0 0.8 copy-start.1
